TPU v7x, 32 devices: a whole 2x2x4 slice. The times are simulated.
32 devices in a mesh: grp: 2 (over x), blk: 16 (over z, y, core).
Axes of the slice: x: 2, y: 2, z: 4, core: 2. Of those that a mesh axis runs over, the one named last changes fastest.
Arguments:
- queries: float32 [16384, 1024], P(('grp', 'blk')), parts along dimension 0, may hold values from -24 to 24
- passages: float32 [16384, 1024], P(('grp', 'blk')), parts along dimension 0, may hold values from -6 to 6
- pattern: int32 [64, 8], P(('grp', 'blk')), parts along dimension 0, may hold values from -1 to 31, as said below
- teacher: bfloat16 [64, 8, 256, 256], P(('grp', 'blk')), parts along dimension 0, may hold values from -20 to 370
Outputs:
- row_loss: float32 [16384], P(('grp', 'blk')), parts along dimension 0
- query_grad: float32 [16384, 1024], P(('grp', 'blk')), parts along dimension 0
- passage_grad: float32 [16384, 1024], P(('grp', 'blk')), parts along dimension 0
There are 2 independent parts, one for each index of `grp`. A program takes and returns all parts, laid end to end along the dimension named above; each array names one. Nothing has to cross between parts.
Inputs may be any that keep to these rules, and one draw needn't show every extreme that they name: Every entry of pattern[g] is -1 or a passage group held by a device of blk within 2 of the device holding query group g, counted around the closed axis; the live entries of a row come first and are distinct; every row has one live entry or more, and some row has 8.
All inputs are finite; a program needn't handle non-finite values.
Results may differ from a plain program's by a relative error of at most 0.0003.
Values sent between devices are 32-bit elements; how exact they have to be, the bound alone decides.
A program may use at most 128 MiB of HBM per device.

v0:
```python
import math

import jax
import jax.numpy as jnp
from jax import lax
from jax.sharding import PartitionSpec as P

REACH = 2


HIGHEST = lax.Precision.HIGHEST


def passed_along(block, axis, distance):
    devices = range(lax.axis_size(axis))
    route = [((i - distance) % len(devices), i) for i in devices]
    return lax.ppermute(block, axis, route)


def body(queries, passages, pattern, teacher):
    groups = pattern.shape[0]
    feature_width = queries.shape[1]
    group_rows = teacher.shape[2]
    held_groups = passages.shape[0] // group_rows
    reach_hops = REACH
    cycle_size = lax.axis_size("blk")
    position = lax.axis_index("blk")
    score_scale = 2.0 / math.sqrt(feature_width)
    from_above = []
    current = passages
    for hop_index in range(reach_hops):
        current = passed_along(current, "blk", -1)
        from_above.append(current)
    from_below = []
    current = passages
    for hop_index in range(reach_hops):
        current = passed_along(current, "blk", 1)
        from_below.append(current)
    window = jnp.stack(from_below[::-1] + [passages] + from_above)
    window = window.reshape((2 * reach_hops + 1) * held_groups, group_rows, feature_width)
    is_live = pattern >= 0
    safe_group = jnp.where(is_live, pattern, 0)
    owner_device = safe_group // held_groups
    within = safe_group % held_groups
    offset = (owner_device - position + reach_hops) % cycle_size
    slot_index = offset * held_groups + within
    chosen = window[slot_index]
    query_rows = queries.reshape(groups, group_rows, feature_width)
    scores = jnp.einsum("grd,gkcd->gkrc", query_rows, chosen, precision=HIGHEST) * score_scale
    live = is_live[:, :, None, None]
    student = jnp.where(live, scores, -jnp.inf)
    top_student = jnp.max(student, axis=(1, 3), keepdims=True)
    exp_student = jnp.exp(student - top_student)
    sum_student = jnp.sum(exp_student, axis=(1, 3), keepdims=True)
    probs = exp_student / sum_student
    log_probs = student - top_student - jnp.log(sum_student)
    logits = jnp.where(live, teacher.astype(jnp.float32), -jnp.inf)
    top_teacher = jnp.max(logits, axis=(1, 3), keepdims=True)
    exp_teacher = jnp.exp(logits - top_teacher)
    sum_teacher = jnp.sum(exp_teacher, axis=(1, 3), keepdims=True)
    target = exp_teacher / sum_teacher
    log_target = logits - top_teacher - jnp.log(sum_teacher)
    terms = jnp.where(live, target * (log_target - log_probs), 0.0)
    row_loss = jnp.sum(terms, axis=(1, 3)).reshape(-1)
    grads = jnp.where(live, probs - target, 0.0) * score_scale
    query_grad = jnp.einsum("gkrc,gkcd->grd", grads, chosen, precision=HIGHEST).reshape(
        -1, feature_width
    )
    tile_grad = jnp.einsum("gkrc,grd->gkcd", grads, query_rows, precision=HIGHEST)
    window_grad = (
        jnp.zeros_like(window)
        .at[slot_index.reshape(-1)]
        .add(tile_grad.reshape(-1, group_rows, feature_width))
    )
    window_grad = window_grad.reshape(2 * reach_hops + 1, held_groups * group_rows, feature_width)
    upward = jnp.zeros_like(passages)
    for hop_index in range(reach_hops, 0, -1):
        upward = passed_along(upward + window_grad[reach_hops + hop_index], "blk", 1)
    downward = jnp.zeros_like(passages)
    for hop_index in range(reach_hops, 0, -1):
        downward = passed_along(downward + window_grad[reach_hops - hop_index], "blk", -1)
    passage_grad = window_grad[reach_hops] + upward + downward
    return (row_loss, query_grad, passage_grad)


def solution(mesh):
    placed = (
        P(("grp", "blk"), None),
        P(("grp", "blk"), None),
        P(("grp", "blk"), None),
        P(("grp", "blk"), None, None, None),
    )
    return jax.shard_map(
        body,
        mesh=mesh,
        in_specs=placed,
        out_specs=(P(("grp", "blk")), P(("grp", "blk"), None), P(("grp", "blk"), None)),
        check_vma=False,
    )
```

profile of v0, /device:TPU:1, one launch (start us, length us, event | category | flops | bytes accessed | tf_op | source)
XLA Modules:
  0.0 301.8 jit_solution(8281802211338831956)
XLA Ops:
  0.6 0.0 copy-start
  0.6 0.0 copy-start.7
  0.7 2.7 collective-permute-start
  3.3 0.0 collective-permute-start.2
  3.3 45.8 %collective-permute-done = f32[512,1024]{1,0:T(8,128)} collective-permute-done((f32[512,1024]{1,0:T(8,128)}, f32[512,1024]{1,0:T(8,128)}, u32[]{:S(2)}, u32[]{:S(2)}) %collective-permute-start) | collective-permute-done | bytes 2097184 | tf_op jit(solution)/shard_map/ppermute | solution.py:17
  49.1 2.5 collective-permute-start.1
  51.6 22.5 %collective-permute-done.2 = f32[512,1024]{1,0:T(8,128)} collective-permute-done((f32[512,1024]{1,0:T(8,128)}, f32[512,1024]{1,0:T(8,128)}, u32[]{:S(2)}, u32[]{:S(2)}) %collective-permute-start.2) | collective-permute-done | bytes 2097184 | tf_op jit(solution)/shard_map/ppermute | solution.py:17
  74.1 0.0 collective-permute-start.3
  74.1 0.7 compare_select_fusion
  74.8 0.1 reshape.84
  74.8 0.1 reshape.80
  74.9 3.9 %copy.7 = bf16[2,8,256,256]{2,3,1,0:T(8,128)(2,1)} copy(bf16[2,8,256,256]{3,2,1,0:T(8,128)(2,1)} %param.7) | data formatting | bytes 4194304 | tf_op args[3]
  78.9 0.0 copy-done.7
  78.9 0.0 copy-start.6
  78.9 17.7 %collective-permute-done.1 = f32[512,1024]{1,0:T(8,128)} collective-permute-done((f32[512,1024]{1,0:T(8,128)}, f32[512,1024]{1,0:T(8,128)}, u32[]{:S(2)}, u32[]{:S(2)}) %collective-permute-start.1) | collective-permute-done | bytes 2097184 | tf_op jit(solution)/shard_map/ppermute | solution.py:17
  96.6 3.2 %bitcast_dynamic-update-slice_fusion.4 = f32[5,512,1024]{2,1,0:T(8,128)} fusion(f32[512,1024]{1,0:T(8,128)} %collective-permute-done.1), kind=kLoop, calls=%fused_computation.23 | loop fusion | bytes 4194304
  99.8 3.1 %bitcast_dynamic-update-slice_fusion.3 = f32[5,512,1024]{2,1,0:T(8,128)} fusion(f32[5,512,1024]{2,1,0:T(8,128)} %bitcast_dynamic-update-slice_fusion.4, f32[512,1024]{1,0:T(8,128)} %collective-permute-done), kind=kLoop, calls=%fused_computation.22 | loop fusion | bytes 4194304
  102.9 0.0 copy-done.6
  102.9 1.4 bitcast_dynamic-update-slice_fusion.2
  104.4 3.2 %bitcast_dynamic-update-slice_fusion.1 = f32[5,512,1024]{2,1,0:T(8,128)} fusion(f32[5,512,1024]{2,1,0:T(8,128)} %bitcast_dynamic-update-slice_fusion.2, f32[512,1024]{1,0:T(8,128)} %collective-permute-done.2), kind=kLoop, calls=%fused_computation.20 | loop fusion | bytes 4194304
  107.5 0.0 collective-permute-done.3
  107.5 3.2 %bitcast_dynamic-update-slice_fusion = f32[5,512,1024]{2,1,0:T(8,128)} fusion(f32[5,512,1024]{2,1,0:T(8,128)} %bitcast_dynamic-update-slice_fusion.1, f32[512,1024]{1,0:T(8,128)} %collective-permute-done.3), kind=kLoop, calls=%fused_computation.19 | loop fusion | bytes 4194304 | tf_op jit(solution)/shard_map/stack | solution.py:39
  110.8 11.9 %gather_fusion = f32[16,256,1024]{2,1,0:T(8,128)} fusion(f32[10,256,1024]{2,1,0:T(8,128)} %bitcast.5, s32[1024]{0:T(1024)S(1)} %pad_clamp_fusion), kind=kCustom, calls=%fused_computation | custom fusion | bytes 33554496 | tf_op jit(solution)/shard_map/gather | solution.py:47
  122.7 0.0 copy-done
  122.7 16.7 %fusion.1 = (f32[2,256]{1,0:T(2,128)S(1)}, f32[2,256]{1,0:T(2,128)S(1)}, f32[2,8,256,256]{3,2,1,0:T(8,128)S(1)}) fusion(bf16[2,8,256,256]{2,3,1,0:T(8,128)(2,1)} %copy.7, pred[2,8]{1,0:T(4,128)(4,1)S(1)} %broadcast_compare_fusion, f32[2,8,256,1024]{3,2,1,0:T(8,128)} %bitcast.55, f32[2,256,1024,1]{2,1,3,0:T(8,128)S(1)} %bitcast.53), kind=kOutput, calls=%fused_computation.9 | convolution fusion | flops 12891192320 | bytes 25169936 | tf_op jit(solution)/shard_map/grd,gkcd->gkrc/dot_general | solution.py:49
  139.4 0.0 copy-start.2
  139.4 1.9 fusion.4
  141.3 17.8 %fusion.12 = f32[2,8,256,1024]{3,2,1,0:T(8,128)} fusion(f32[2,256,1024,1]{2,1,3,0:T(8,128)S(1)} %bitcast.54, bf16[2,8,256,256]{2,3,1,0:T(8,128)(2,1)S(1)} %copy-done.4, f32[2,8,256,256]{3,2,1,0:T(8,128)S(1)} %get-tuple-element.14, f32[2,256]{1,0:T(2,128)S(1)} %get-tuple-element.4, f32[2,256]{1,0:T(2,128)S(1)} %get-tuple-element.6, ...), kind=kOutput, calls=%fused_computation.40 | convolution fusion | flops 12896436224 | bytes 25174032 | tf_op jit(solution)/shard_map/gkrc,grd->gkcd/dot_general | solution.py:69
  159.1 5.3 %broadcast_in_dim.44 = f32[10,256,1024]{2,1,0:T(8,128)} broadcast(f32[]{:T(128)} %constant.46.clone.1), dimensions={} | broadcast | bytes 10485764 | tf_op jit(solution)/shard_map/broadcast_in_dim | solution.py:71
  164.4 33.3 %scatter_fusion = f32[10,256,1024]{2,1,0:T(8,128)} fusion(f32[10,256,1024]{2,1,0:T(8,128)} %broadcast_in_dim.44, s32[16]{0:T(128)S(1)} %fusion.11, f32[16,256,1024]{2,1,0:T(8,128)} %bitcast.57), kind=kCustom, calls=%fused_computation.1 | custom fusion | flops 4194304 | bytes 50331712 | tf_op jit(solution)/shard_map/scatter-add | solution.py:73
  197.6 5.5 %fusion.15 = (f32[2,256,1024]{2,1,0:T(8,128)S(1)}, f32[2,256,1024]{2,1,0:T(8,128)S(1)}, f32[2,256,1024]{2,1,0:T(8,128)S(1)}, f32[2,256,1024]{2,1,0:T(8,128)S(1)}, f32[2,256,1024]{2,1,0:T(8,128)S(1)}) fusion(f32[10,256,1024]{2,1,0:T(8,128)} %scatter_fusion), kind=kLoop, calls=%fused_computation.42 | loop fusion | bytes 20971520 | tf_op jit(solution)/shard_map/slice | solution.py:82
  203.2 0.1 collective-permute-start.6
  203.2 2.0 collective-permute-start.4
  205.2 46.1 %collective-permute-done.6 = f32[512,1024]{1,0:T(8,128)S(1)} collective-permute-done((f32[512,1024]{1,0:T(8,128)S(1)}, f32[512,1024]{1,0:T(8,128)S(1)}, u32[]{:S(2)}, u32[]{:S(2)}) %collective-permute-start.6) | collective-permute-done | bytes 2097184 | tf_op jit(solution)/shard_map/ppermute | solution.py:17
  251.3 0.4 bitcast_add_fusion
  251.8 0.0 copy-start.5
  251.8 0.1 collective-permute-start.7
  251.8 0.0 collective-permute-done.4
  251.8 0.4 bitcast_add_fusion.1
  252.3 1.8 collective-permute-start.5
  254.1 0.0 copy-done.3
  254.1 0.6 copy-done.5
  254.6 2.2 select_reduce_fusion
  256.9 0.6 copy.19
  257.4 22.1 %fusion.13 = f32[2,256,1024,1]{2,1,3,0:T(8,128)} fusion(f32[2,8,256,1024]{3,2,1,0:T(8,128)} %bitcast.56, bf16[2,8,256,256]{2,3,1,0:T(8,128)(2,1)S(1)} %copy-done.5, f32[2,8,256,256]{3,2,1,0:T(8,128)S(1)} %copy-done.3, f32[2,256]{1,0:T(2,128)S(1)} %get-tuple-element.4, f32[2,256]{1,0:T(2,128)S(1)} %get-tuple-element.6, f32[2,256]{1,0:T(2,128)S(1)} %get-tuple-element.3, ...), kind=kOutput, calls=%fused_computation.41 | convolution fusion | flops 12896436224 | bytes 25174032 | tf_op jit(solution)/shard_map/gkrc,gkcd->grd/dot_general | solution.py:66
  279.6 20.2 %collective-permute-done.7 = f32[512,1024]{1,0:T(8,128)S(1)} collective-permute-done((f32[512,1024]{1,0:T(8,128)S(1)}, f32[512,1024]{1,0:T(8,128)S(1)}, u32[]{:S(2)}, u32[]{:S(2)}) %collective-permute-start.7) | collective-permute-done | bytes 2097184 | tf_op jit(solution)/shard_map/ppermute | solution.py:17
  299.8 0.0 collective-permute-done.5
  299.8 2.0 fusion.7
  (11 shorter events, 0.0 us)
Async XLA Ops:
  0.6 122.0 %copy-start = (f32[512,1024]{1,0:T(8,128)S(1)}, f32[512,1024]{1,0:T(8,128)}, u32[]{:S(2)}) copy-start(f32[512,1024]{1,0:T(8,128)} %param.4) | copy-start | bytes 6291460
  0.6 78.2 %copy-start.7 = (s32[2,8]{1,0:T(2,128)S(1)}, s32[2,8]{1,0:T(2,128)}, u32[]{:S(2)}) copy-start(s32[2,8]{1,0:T(2,128)} %param.6) | copy-start | bytes 196
  0.7 48.4 %collective-permute-start = (f32[512,1024]{1,0:T(8,128)}, f32[512,1024]{1,0:T(8,128)}, u32[]{:S(2)}, u32[]{:S(2)}) collective-permute-start(f32[512,1024]{1,0:T(8,128)} %param.5), channel_id=1, source_target_pairs={{15,0},{0,1},{1,2},{2,3},{3,4},{4,5},{5,6},{6,7},{7,8},{8,9},{9,10... | collective-permute-start | bytes 6291464 | tf_op jit(solution)/shard_map/ppermute | solution.py:17
  3.3 70.7 %collective-permute-start.2 = (f32[512,1024]{1,0:T(8,128)}, f32[512,1024]{1,0:T(8,128)}, u32[]{:S(2)}, u32[]{:S(2)}) collective-permute-start(f32[512,1024]{1,0:T(8,128)} %param.5), channel_id=1, source_target_pairs={{1,0},{2,1},{3,2},{4,3},{5,4},{6,5},{7,6},{8,7},{9,8},{10,9},{11,1... | collective-permute-start | bytes 6291464 | tf_op jit(solution)/shard_map/ppermute | solution.py:17
  49.1 47.5 %collective-permute-start.1 = (f32[512,1024]{1,0:T(8,128)}, f32[512,1024]{1,0:T(8,128)}, u32[]{:S(2)}, u32[]{:S(2)}) collective-permute-start(f32[512,1024]{1,0:T(8,128)} %collective-permute-done), channel_id=1, source_target_pairs={{15,0},{0,1},{1,2},{2,3},{3,4},{4,5},{5,6},{6,7},{7,8},{8,9},{9,10... | collective-permute-start | bytes 6291464 | tf_op jit(solution)/shard_map/ppermute | solution.py:17
  74.1 33.5 %collective-permute-start.3 = (f32[512,1024]{1,0:T(8,128)}, f32[512,1024]{1,0:T(8,128)}, u32[]{:S(2)}, u32[]{:S(2)}) collective-permute-start(f32[512,1024]{1,0:T(8,128)} %collective-permute-done.2), channel_id=1, source_target_pairs={{1,0},{2,1},{3,2},{4,3},{5,4},{6,5},{7,6},{8,7},{9,8},{10,9},{11,1... | collective-permute-start | bytes 6291464 | tf_op jit(solution)/shard_map/ppermute | solution.py:17
  78.9 24.0 %copy-start.6 = (f32[512,1024]{1,0:T(8,128)S(1)}, f32[512,1024]{1,0:T(8,128)}, u32[]{:S(2)}) copy-start(f32[512,1024]{1,0:T(8,128)} %param.5) | copy-start | bytes 6291460
  122.7 16.7 %copy-start.4 = (bf16[2,8,256,256]{2,3,1,0:T(8,128)(2,1)S(1)}, bf16[2,8,256,256]{2,3,1,0:T(8,128)(2,1)}, u32[]{:S(2)}) copy-start(bf16[2,8,256,256]{2,3,1,0:T(8,128)(2,1)} %copy.7) | copy-start | bytes 6291460
  139.4 19.7 %copy-start.2 = (f32[2,8,256,256]{3,2,1,0:T(8,128)}, f32[2,8,256,256]{3,2,1,0:T(8,128)S(1)}, u32[]{:S(2)}) copy-start(f32[2,8,256,256]{3,2,1,0:T(8,128)S(1)} %get-tuple-element.14) | copy-start | bytes 12582916
  203.2 48.2 %collective-permute-start.6 = (f32[512,1024]{1,0:T(8,128)S(1)}, f32[512,1024]{1,0:T(8,128)S(1)}, u32[]{:S(2)}, u32[]{:S(2)}) collective-permute-start(f32[512,1024]{1,0:T(8,128)S(1)} %bitcast.59), channel_id=1, source_target_pairs={{1,0},{2,1},{3,2},{4,3},{5,4},{6,5},{7,6},{8,7},{9,8},{10,9},{11,1... | collective-permute-start | bytes 6291464 | tf_op jit(solution)/shard_map/ppermute | solution.py:17
  203.2 48.6 %collective-permute-start.4 = (f32[512,1024]{1,0:T(8,128)S(1)}, f32[512,1024]{1,0:T(8,128)S(1)}, u32[]{:S(2)}, u32[]{:S(2)}) collective-permute-start(f32[512,1024]{1,0:T(8,128)S(1)} %bitcast.58), channel_id=1, source_target_pairs={{15,0},{0,1},{1,2},{2,3},{3,4},{4,5},{5,6},{6,7},{7,8},{8,9},{9,10... | collective-permute-start | bytes 6291464 | tf_op jit(solution)/shard_map/ppermute | solution.py:17
  251.8 2.3 copy-start.3
  251.8 2.9 copy-start.5
  251.8 48.0 %collective-permute-start.7 = (f32[512,1024]{1,0:T(8,128)S(1)}, f32[512,1024]{1,0:T(8,128)S(1)}, u32[]{:S(2)}, u32[]{:S(2)}) collective-permute-start(f32[512,1024]{1,0:T(8,128)S(1)} %bitcast_add_fusion), channel_id=1, source_target_pairs={{1,0},{2,1},{3,2},{4,3},{5,4},{6,5},{7,6},{8,7},{9,8},{10,9},{11,1... | collective-permute-start | bytes 6291464 | tf_op jit(solution)/shard_map/ppermute | solution.py:17
  252.3 47.5 %collective-permute-start.5 = (f32[512,1024]{1,0:T(8,128)S(1)}, f32[512,1024]{1,0:T(8,128)S(1)}, u32[]{:S(2)}, u32[]{:S(2)}) collective-permute-start(f32[512,1024]{1,0:T(8,128)S(1)} %bitcast_add_fusion.1), channel_id=1, source_target_pairs={{15,0},{0,1},{1,2},{2,3},{3,4},{4,5},{5,6},{6,7},{7,8},{8,9},{9,10... | collective-permute-start | bytes 6291464 | tf_op jit(solution)/shard_map/ppermute | solution.py:17
  299.8 2.0 copy-start.1
where the time goes:
time: 305 us; the launch traced here: 302 us
  waiting for transfers between devices  152 us (50%)
  matrix products  56.6 us (19%)
  local copies, waits for them, and re-layouts  42.2 us (14%)
  other arithmetic  40.9 us (13%)
  starting transfers between devices  9.03 us (3%)
    ppermute x8, waiting for transfers between devices, passed_along(): return lax.ppermute(block, axis, route)  152 us
    scatter-add x1, other arithmetic, body(): window_grad = jnp.zeros_like(window).at[slot_index.reshape(-1)].add(tile_...  33.3 us
    dot_general x1, matrix products, body(): jnp.einsum('gkrc,gkcd->grd', grads, chosen, precision=HIGHEST)  22.1 us
    dot_general x1, matrix products, body(): jnp.einsum('gkrc,grd->gkcd', grads, query_rows, precision=HIGHEST)  17.8 us
    dot_general x1, matrix products, body(): jnp.einsum('grd,gkcd->gkrc', query_rows, chosen, precision=HIGHEST)  16.7 us
    unnamed x22, local copies, waits for them, and re-layouts  16.1 us
    gather x1, local copies, waits for them, and re-layouts, body(): chosen = window[slot_index]  11.9 us
    ppermute x8, starting transfers between devices, passed_along(): return lax.ppermute(block, axis, route)  9.03 us
  transfers between devices with their start and end apart: 8, of which 5 were waited for; matrix products, arithmetic and copies ran while one was open for 14% of the time, Pallas kernels for 0%

commit v1 on v0

v1 whole, which is shorter than its diff:
```python
import functools
import math

import jax
import jax.numpy as jnp
from jax import lax
from jax.experimental import pallas as pl
from jax.experimental.pallas import tpu as pltpu
from jax.sharding import PartitionSpec as P

CHUNKS = 8
DEAD = -1e30
SIB, YB, ZB, FB, OWN = range(5)
F32 = jnp.float32
BF16 = jnp.bfloat16
MESH = pl.DeviceIdType.MESH


def split(x):
    hi = x.astype(BF16)
    return hi, (x - hi.astype(F32)).astype(BF16)


def dot(a, b, ca, cb):
    return lax.dot_general(a, b, (((ca,), (cb,)), ((), ())), preferred_element_type=F32)


def dot3(ah, al, bh, bl, ca, cb):
    return dot(ah, bh, ca, cb) + (dot(al, bh, ca, cb) + dot(ah, bl, ca, cb))


def fold(x, op):
    rows, cols = x.shape
    return op(x.reshape(rows // 8, 8, cols), axis=0)


def kernel(
    n, pat, q, p, teach, loss, qg, pg,
    win, wh, wl, qh, ql, st, tg, gh, gl, rec, stat, kk, cap,
    s1, r1, s2, r2,
):
    rows, width = q.shape
    groups, slots, size, _ = teach.shape
    scale = 2.0 / math.sqrt(width)
    part = lax.axis_index("grp")
    me = lax.axis_index("blk")
    chip, core = me // 2, me % 2
    odd = chip % 2
    to = 1 - 2 * odd
    wrap = lambda i: lax.rem(i + n, n)
    sib = me + 1 - 2 * core
    ypart = me + 2 * to
    znext = wrap(me + 4 * to)
    zprev = wrap(me - 4 * to)
    owners = [sib, ypart, wrap(me - 2 * to), wrap(me + 2 * core - 1), me]
    fwd_y = core == odd
    z_gets = core != odd

    barrier = pltpu.get_barrier_semaphore()
    for d in (sib, ypart, znext, zprev):
        pl.semaphore_signal(barrier, inc=1, device_id=(part, d), device_id_type=MESH)
    pl.semaphore_wait(barrier, 4)

    def copy(src, dst, ss, rs, kind, i, dev):
        return pltpu.make_async_remote_copy(
            src_ref=src, dst_ref=dst, send_sem=ss.at[kind, i], recv_sem=rs.at[kind, i],
            device_id=(part, dev), device_id_type=MESH,
        )

    step = rows // CHUNKS
    half = CHUNKS // 2
    piece = lambda i: pl.ds(i * step, step)
    group = lambda j: pl.ds(j * size, size)

    g_sib = lambda i: copy(p.at[piece(i)], win.at[SIB, piece(i)], s1, r1, SIB, i, sib)
    g_y = lambda i: copy(p.at[piece(i)], win.at[YB, piece(i)], s1, r1, YB, i, ypart)
    g_z = lambda i: copy(win.at[YB, piece(i)], win.at[ZB, piece(i)], s1, r1, ZB, i, znext)
    g_f = lambda b, i: copy(win.at[b, piece(i)], win.at[FB, piece(i)], s1, r1, FB, i, sib)
    t_sib = lambda i: copy(win.at[SIB, piece(i)], rec.at[SIB, piece(i)], s2, r2, SIB, i, sib)
    t_y = lambda i: copy(win.at[YB, piece(i)], rec.at[YB, piece(i)], s2, r2, YB, i, ypart)
    t_z = lambda i: copy(win.at[ZB, piece(i)], rec.at[ZB, piece(i)], s2, r2, ZB, i, zprev)
    t_f = lambda i: copy(win.at[FB, piece(i)], rec.at[FB, piece(i)], s2, r2, FB, i, sib)

    for i in range(CHUNKS):
        g_y(i).start()
    for i in range(CHUNKS):
        g_sib(i).start()

    for b in range(5):
        for j in range(2):
            wanted = owners[b] * 2 + j
            for g in range(groups):
                slot, live = jnp.int32(0), jnp.int32(0)
                for k in range(slots):
                    hit = (pat[g, k] == wanted).astype(jnp.int32)
                    slot = jnp.maximum(slot, hit * k)
                    live = jnp.maximum(live, hit)
                kk[(g * 5 + b) * 2 + j] = slot
                alive = live.astype(F32)
                cap[(g * 5 + b) * 2 + j] = 3e38 * alive + DEAD * (1.0 - alive)

    stat[...] = jnp.full(stat.shape, DEAD, F32)

    def split_rows(src, hi, lo, count, strip=32):
        def one(t, _):
            r = pl.ds(pl.multiple_of(t * strip, strip), strip)
            h, l = split(src[r, :])
            hi[r, :] = h
            lo[r, :] = l
            return 0
        lax.fori_loop(0, count // strip, one, 0)

    def score(b, j):
        src = p.at[group(j)] if b == OWN else win.at[b, group(j)]
        split_rows(src, wh.at[b, group(j)], wl.at[b, group(j)], size)
        for g in range(groups):
            cols = pl.ds(g * size, size)
            s = dot3(wh[b, group(j), :], wl[b, group(j), :], qh[group(g), :], ql[group(g), :], 1, 1)
            s = jnp.minimum(s * scale, cap[(g * 5 + b) * 2 + j])
            st[b, group(j), cols] = s
            stat[0:8, cols] = jnp.maximum(stat[0:8, cols], fold(s, jnp.max))

    def teacher(b):
        def one(t, _):
            g, j = t // 2, t % 2
            at = (g * 5 + b) * 2 + j
            x = teach[g, kk[at]].astype(F32).T
            x = jnp.minimum(x, cap[at])
            r = pl.ds(pl.multiple_of(j * size, size), size)
            c = pl.ds(pl.multiple_of(g * size, size), size)
            tg[b, r, c] = x
            stat[8:16, c] = jnp.maximum(stat[8:16, c], fold(x, jnp.max))
            return 0
        lax.fori_loop(0, groups * 2, one, 0)

    strip = 64
    per = rows // strip

    def teacher_sums(lo, hi, top):
        def one(t, carry):
            z, d = carry
            r = pl.ds(pl.multiple_of((t % per) * strip, strip), strip)
            x = tg[t // per, r, :] - top
            e = jnp.exp(x)
            tg[t // per, r, :] = e
            return z + fold(e, jnp.sum), d + fold(e * x, jnp.sum)
        zero = jnp.zeros((8, rows), F32)
        z, d = lax.fori_loop(lo * per, hi * per, one, (zero, zero))
        stat[16:24, :] = z
        stat[24:32, :] = d

    def all_teacher():
        teacher_sums(0, 5, jnp.max(stat[8:16, :], axis=0, keepdims=True))

    work = [
        lambda: (split_rows(q, qh, ql, rows), score(OWN, 0)),
        lambda: (score(OWN, 1), [g_sib(i).wait_recv() for i in range(CHUNKS)]),
        lambda: score(SIB, 0),
        lambda: (score(SIB, 1), teacher(0)),
        lambda: (teacher(1), teacher(2)),
        lambda: teacher(3),
        lambda: teacher(4),
        all_teacher,
    ]
    per_step = -(-len(work) // CHUNKS)
    for i in range(CHUNKS + 1):
        if i < CHUNKS:
            g_y(i).wait_recv()
            g_z(i).start()

            @pl.when(fwd_y)
            def _():
                g_f(YB, i).start()

        if i >= 1:
            g_z(i - 1).wait_recv()

            @pl.when(jnp.logical_not(fwd_y))
            def _():
                g_f(ZB, i - 1).start()

        for f in work[i * per_step:(i + 1) * per_step]:
            f()
        if i == half - 1:
            score(YB, 0)
        if i == half:
            score(ZB, 0)
        if i == half + 1:
            for a in range(half):
                g_f(YB, a).wait_recv()
            score(FB, 0)
        if i == CHUNKS - 1:
            score(YB, 1)
    score(ZB, 1)
    for a in range(half, CHUNKS):
        g_f(YB, a).wait_recv()
    score(FB, 1)
    for i in range(CHUNKS):
        g_y(i).wait_send()
        g_sib(i).wait_send()
        g_z(i).wait_send()
        g_f(YB, i).wait_send()

    top = jnp.max(stat[0:8, :], axis=0, keepdims=True)

    def one(t, carry):
        z, d = carry
        r = pl.ds(pl.multiple_of((t % per) * strip, strip), strip)
        x = st[t // per, r, :] - top
        e = jnp.exp(x)
        st[t // per, r, :] = e
        return z + fold(e, jnp.sum), d + fold(tg[t // per, r, :] * x, jnp.sum)

    zero = jnp.zeros((8, rows), F32)
    zs, cross = lax.fori_loop(0, 5 * per, one, (zero, zero))
    zs = jnp.sum(zs, axis=0, keepdims=True)
    cross = jnp.sum(cross, axis=0, keepdims=True)
    zt = jnp.sum(stat[16:24, :], axis=0, keepdims=True)
    dt = jnp.sum(stat[24:32, :], axis=0, keepdims=True)
    loss[...] = (dt - cross) / zt - jnp.log(zt) + jnp.log(zs)
    ks, kt = scale / zs, scale / zt

    def make_grads(b, j):
        def one(t, _):
            r = pl.ds(pl.multiple_of(j * size + t * 64, 64), 64)
            h, l = split(st[b, r, :] * ks - tg[b, r, :] * kt)
            gh[b, r, :] = h
            gl[b, r, :] = l
            return 0
        lax.fori_loop(0, size // 64, one, 0)

    def weigh(b, j):
        make_grads(b, j)
        out = pg.at[group(j)] if b == OWN else win.at[b, group(j)]

        def one(t, _):
            c = pl.ds(pl.multiple_of(t * 256, 256), 256)
            out[:, c] = dot3(gh[b, group(j), :], gl[b, group(j), :], qh[:, c], ql[:, c], 1, 0)
            return 0
        lax.fori_loop(0, width // 256, one, 0)

    def add(dst, src, start, count):
        def one(t, _):
            r = pl.ds(pl.multiple_of(start + t * 16, 16), 16)
            dst[r, :] = dst[r, :] + src[r, :]
            return 0
        lax.fori_loop(0, count // 16, one, 0)

    for j in range(2):
        mine = range(j * half, (j + 1) * half)
        weigh(FB, j)
        for i in mine:
            t_f(i).start()
        weigh(ZB, j)

        @pl.when(z_gets)
        def _():
            for i in mine:
                t_f(i).wait_recv()
            add(win.at[ZB], rec.at[FB], j * size, size)

        for i in mine:
            t_z(i).start()
    for j in range(2):
        mine = range(j * half, (j + 1) * half)
        weigh(YB, j)

        @pl.when(jnp.logical_not(z_gets))
        def _():
            for i in mine:
                t_f(i).wait_recv()
            add(win.at[YB], rec.at[FB], j * size, size)

    def query_part(b, m):
        def one(t, _):
            c = pl.ds(pl.multiple_of(t * 256, 256), 256)
            x = dot3(gh[b, :, group(m)], gl[b, :, group(m)], wh[b, :, c], wl[b, :, c], 0, 0)
            if b == SIB:
                qg[group(m), c] = x
            else:
                qg[group(m), c] = qg[group(m), c] + x
            return 0
        lax.fori_loop(0, width // 256, one, 0)

    def sibling_out():
        for j in range(2):
            weigh(SIB, j)
            for i in range(j * half, (j + 1) * half):
                t_sib(i).start()

    def own_out():
        for j in range(2):
            weigh(OWN, j)

    def sibling_in():
        for i in range(CHUNKS):
            t_sib(i).wait_recv()
        add(pg, rec.at[SIB], 0, rows)

    work = [sibling_out, own_out] + [
        functools.partial(query_part, b, m) for b in range(5) for m in range(2)
    ]
    work.insert(4, sibling_in)
    per_step = -(-len(work) // CHUNKS)
    for i in range(CHUNKS + 1):
        if i < CHUNKS:
            t_z(i).wait_recv()
            add(win.at[YB], rec.at[ZB], i * step, step)
            t_y(i).start()
        for f in work[i * per_step:(i + 1) * per_step]:
            f()
        if i >= 1:
            t_y(i - 1).wait_recv()
            add(pg, rec.at[YB], (i - 1) * step, step)
    for i in range(CHUNKS):
        t_sib(i).wait_send()
        t_f(i).wait_send()
        t_z(i).wait_send()
        t_y(i).wait_send()


def body(n, queries, passages, pattern, teacher):
    rows, width = queries.shape
    vmem = pl.BlockSpec(memory_space=pltpu.VMEM)
    loss, query_grad, passage_grad = pl.pallas_call(
        functools.partial(kernel, n),
        out_shape=(
            jax.ShapeDtypeStruct((1, rows), F32),
            jax.ShapeDtypeStruct((rows, width), F32),
            jax.ShapeDtypeStruct((rows, width), F32),
        ),
        in_specs=[pl.BlockSpec(memory_space=pltpu.SMEM), vmem, vmem, vmem],
        out_specs=(vmem, vmem, vmem),
        scratch_shapes=[
            pltpu.VMEM((4, rows, width), F32),
            pltpu.VMEM((5, rows, width), BF16),
            pltpu.VMEM((5, rows, width), BF16),
            pltpu.VMEM((rows, width), BF16),
            pltpu.VMEM((rows, width), BF16),
            pltpu.VMEM((5, rows, rows), F32),
            pltpu.VMEM((5, rows, rows), F32),
            pltpu.VMEM((5, rows, rows), BF16),
            pltpu.VMEM((5, rows, rows), BF16),
            pltpu.VMEM((4, rows, width), F32),
            pltpu.VMEM((32, rows), F32),
            pltpu.SMEM((20,), jnp.int32),
            pltpu.SMEM((20,), F32),
            pltpu.SemaphoreType.DMA((4, CHUNKS)),
            pltpu.SemaphoreType.DMA((4, CHUNKS)),
            pltpu.SemaphoreType.DMA((4, CHUNKS)),
            pltpu.SemaphoreType.DMA((4, CHUNKS)),
        ],
        compiler_params=pltpu.CompilerParams(
            collective_id=0, has_side_effects=True, vmem_limit_bytes=60 * 2**20
        ),
    )(pattern, queries, passages, teacher)
    return loss.reshape(rows), query_grad, passage_grad


def solution(mesh):
    placed = (
        P(("grp", "blk"), None),
        P(("grp", "blk"), None),
        P(("grp", "blk"), None),
        P(("grp", "blk"), None, None, None),
    )
    return jax.shard_map(
        functools.partial(body, mesh.shape["blk"]),
        mesh=mesh,
        in_specs=placed,
        out_specs=(P(("grp", "blk")), P(("grp", "blk"), None), P(("grp", "blk"), None)),
        check_vma=False,
    )
```

time: 305 us -> 135 us (0.44)
  waiting for transfers between devices: 152 us -> 0 us
  Pallas kernels: 0 us -> 127 us
  matrix products: 56.6 us -> 0 us
  other arithmetic: 40.9 us -> 0 us
  local copies, waits for them, and re-layouts: 42.2 us -> 5.88 us
  starting transfers between devices: 9.03 us -> 0 us
    ppermute x8 -> x0, waiting for transfers between devices: 152 us -> none  [passed_along(): return lax.ppermute(block, axis, route)]
    pallas_call x0 -> x1, Pallas kernels: none -> 127 us  [body(): pl.pallas_call(functools.partial(kernel, n), out_shape=(jax.ShapeDtypeStr...]
    dot_general x3 -> x0, matrix products: 56.6 us -> none  [the longest x1 22.1 us: body(): jnp.einsum('gkrc,gkcd->grd', grads, chosen, precision=HIGHEST)]
    scatter-add x1 -> x0, other arithmetic: 33.3 us -> none  [body(): window_grad = jnp.zeros_like(window).at[slot_index.reshape(-1)].add(tile_...]
    gather x1 -> x0, local copies, waits for them, and re-layouts: 11.9 us -> none  [body(): chosen = window[slot_index]]
    unnamed x22 -> x5, local copies, waits for them, and re-layouts: 16.1 us -> 5.88 us
    ppermute x8 -> x0, starting transfers between devices: 9.03 us -> none  [passed_along(): return lax.ppermute(block, axis, route)]
    slice x1 -> x0, local copies, waits for them, and re-layouts: 5.5 us -> none  [body(): passage_grad = window_grad[reach_hops] + upward + downward]
  transfers between devices with their start and end apart: 8 -> 0, of which waited for: 5 -> 0; matrix products, arithmetic and copies ran while one was open for 14% -> 0% of each run, Pallas kernels for 0% -> 0%
where the time goes in v1:
time: 135 us; the launch traced here: 133 us
  Pallas kernels  127 us (94%)
  local copies, waits for them, and re-layouts  5.88 us (4%)
    pallas_call x1, Pallas kernels, body(): pl.pallas_call(functools.partial(kernel, n), out_shape=(jax.ShapeDtypeStr...  127 us
    unnamed x5, local copies, waits for them, and re-layouts  5.88 us

profile of v1, /device:TPU:1, one launch (start us, length us, event | category | flops | bytes accessed | tf_op | source)
XLA Modules:
  0.0 133.3 jit_solution(5696278770871045665)
XLA Ops:
  0.6 126.7 %shard_map.67 = (f32[1,512]{1,0:T(1,128)}, f32[512,1024]{1,0:T(8,128)}, f32[512,1024]{1,0:T(8,128)}) custom-call(s32[2,8]{1,0:T(2,128)} %pat.1, f32[512,1024]{1,0:T(8,128)} %q.1, f32[512,1024]{1,0:T(8,128)} %p.1, bf16[2,8,256,256]{3,2,1,0:T(8,128)(2,1)} %teach.1), custom_call_target="tpu_custom_call" | custom-call | tf_op jit(solution)/shard_map/pallas_call | solution.py:325
  127.4 1.3 copy.10
  128.6 0.0 copy-start
  128.6 3.3 %copy.11 = f32[512,1024]{1,0:T(8,128)} copy(f32[512,1024]{1,0:T(8,128)} %get-tuple-element.13) | data formatting | bytes 4194304
  131.9 0.0 copy-done
  132.0 1.3 copy.12
Async XLA Ops:
  128.6 3.3 %copy-start = (f32[512,1024]{1,0:T(8,128)S(1)}, f32[512,1024]{1,0:T(8,128)}, u32[]{:S(2)}) copy-start(f32[512,1024]{1,0:T(8,128)} %get-tuple-element.14) | copy-start | bytes 6291460

commit v2 on v1

--- a/solution.py
+++ b/solution.py
@@ -9,6 +9,7 @@
 from jax.sharding import PartitionSpec as P
 
 CHUNKS = 8
+BANDS = 2
 DEAD = -1e30
 SIB, YB, ZB, FB, OWN = range(5)
 F32 = jnp.float32
@@ -35,9 +36,10 @@
 
 
 def kernel(
-    n, pat, q, p, teach, loss, qg, pg,
+    n, pat, qin, pin, tin, loss, qout, pout,
+    q, p, teach, qg, pg,
     win, wh, wl, qh, ql, st, tg, gh, gl, rec, stat, kk, cap,
-    s1, r1, s2, r2,
+    s1, r1, s2, r2, ins, outs,
 ):
     rows, width = q.shape
     groups, slots, size, _ = teach.shape
@@ -56,6 +58,9 @@
     fwd_y = core == odd
     z_gets = core != odd
 
+    for i, (a, b) in enumerate(((pin, p), (qin, q), (tin, teach))):
+        pltpu.make_async_copy(a, b, ins.at[i]).start()
+
     barrier = pltpu.get_barrier_semaphore()
     for d in (sib, ypart, znext, zprev):
         pl.semaphore_signal(barrier, inc=1, device_id=(part, d), device_id_type=MESH)
@@ -68,12 +73,15 @@
         )
 
     step = rows // CHUNKS
-    half = CHUNKS // 2
+    quarter = CHUNKS // BANDS
     piece = lambda i: pl.ds(i * step, step)
     group = lambda j: pl.ds(j * size, size)
-
-    g_sib = lambda i: copy(p.at[piece(i)], win.at[SIB, piece(i)], s1, r1, SIB, i, sib)
-    g_y = lambda i: copy(p.at[piece(i)], win.at[YB, piece(i)], s1, r1, YB, i, ypart)
+    band = rows // BANDS
+    rows_of = lambda t: pl.ds(t * band, band)
+    loaded = lambda i, a, b: pltpu.make_async_copy(a, b, ins.at[i]).wait()
+
+    g_sib = lambda i: copy(pin.at[piece(i)], win.at[SIB, piece(i)], s1, r1, SIB, i, sib)
+    g_y = lambda i: copy(pin.at[piece(i)], win.at[YB, piece(i)], s1, r1, YB, i, ypart)
     g_z = lambda i: copy(win.at[YB, piece(i)], win.at[ZB, piece(i)], s1, r1, ZB, i, znext)
     g_f = lambda b, i: copy(win.at[b, piece(i)], win.at[FB, piece(i)], s1, r1, FB, i, sib)
     t_sib = lambda i: copy(win.at[SIB, piece(i)], rec.at[SIB, piece(i)], s2, r2, SIB, i, sib)
@@ -110,59 +118,71 @@
             return 0
         lax.fori_loop(0, count // strip, one, 0)
 
-    def score(b, j):
-        src = p.at[group(j)] if b == OWN else win.at[b, group(j)]
-        split_rows(src, wh.at[b, group(j)], wl.at[b, group(j)], size)
+    def score(b, t):
+        j = t * band // size
+        src = p.at[rows_of(t)] if b == OWN else win.at[b, rows_of(t)]
+        split_rows(src, wh.at[b, rows_of(t)], wl.at[b, rows_of(t)], band)
         for g in range(groups):
             cols = pl.ds(g * size, size)
-            s = dot3(wh[b, group(j), :], wl[b, group(j), :], qh[group(g), :], ql[group(g), :], 1, 1)
+            s = dot3(wh[b, rows_of(t), :], wl[b, rows_of(t), :], qh[group(g), :], ql[group(g), :], 1, 1)
             s = jnp.minimum(s * scale, cap[(g * 5 + b) * 2 + j])
-            st[b, group(j), cols] = s
+            st[b, rows_of(t), cols] = s
             stat[0:8, cols] = jnp.maximum(stat[0:8, cols], fold(s, jnp.max))
 
-    def teacher(b):
-        def one(t, _):
-            g, j = t // 2, t % 2
+    def teacher(b, g):
+        def one(j, _):
             at = (g * 5 + b) * 2 + j
             x = teach[g, kk[at]].astype(F32).T
             x = jnp.minimum(x, cap[at])
             r = pl.ds(pl.multiple_of(j * size, size), size)
-            c = pl.ds(pl.multiple_of(g * size, size), size)
+            c = pl.ds(g * size, size)
             tg[b, r, c] = x
             stat[8:16, c] = jnp.maximum(stat[8:16, c], fold(x, jnp.max))
             return 0
-        lax.fori_loop(0, groups * 2, one, 0)
+        lax.fori_loop(0, 2, one, 0)
 
     strip = 64
     per = rows // strip
 
-    def teacher_sums(lo, hi, top):
+    def teacher_sums(b):
+        top = jnp.max(stat[8:16, :], axis=0, keepdims=True)
+
         def one(t, carry):
             z, d = carry
-            r = pl.ds(pl.multiple_of((t % per) * strip, strip), strip)
-            x = tg[t // per, r, :] - top
+            r = pl.ds(pl.multiple_of(t * strip, strip), strip)
+            x = tg[b, r, :] - top
             e = jnp.exp(x)
-            tg[t // per, r, :] = e
+            tg[b, r, :] = e
             return z + fold(e, jnp.sum), d + fold(e * x, jnp.sum)
         zero = jnp.zeros((8, rows), F32)
-        z, d = lax.fori_loop(lo * per, hi * per, one, (zero, zero))
+        z, d = lax.fori_loop(0, per, one, (zero, zero))
+        if b:
+            z, d = stat[16:24, :] + z, stat[24:32, :] + d
         stat[16:24, :] = z
         stat[24:32, :] = d
 
-    def all_teacher():
-        teacher_sums(0, 5, jnp.max(stat[8:16, :], axis=0, keepdims=True))
-
-    work = [
-        lambda: (split_rows(q, qh, ql, rows), score(OWN, 0)),
-        lambda: (score(OWN, 1), [g_sib(i).wait_recv() for i in range(CHUNKS)]),
-        lambda: score(SIB, 0),
-        lambda: (score(SIB, 1), teacher(0)),
-        lambda: (teacher(1), teacher(2)),
-        lambda: teacher(3),
-        lambda: teacher(4),
-        all_teacher,
-    ]
-    per_step = -(-len(work) // CHUNKS)
+    def first():
+        loaded(0, pin, p)
+        loaded(1, qin, q)
+        split_rows(q, qh, ql, rows)
+
+    def sibling():
+        for i in range(CHUNKS):
+            g_sib(i).wait_recv()
+        score(SIB, 0)
+
+    work = [first] + [functools.partial(score, OWN, t) for t in range(BANDS)]
+    work += [sibling] + [functools.partial(score, SIB, t) for t in range(1, BANDS)]
+    work += [lambda: loaded(2, tin, teach)]
+    work += [functools.partial(teacher, b, g) for b in range(5) for g in range(groups)]
+    work += [functools.partial(teacher_sums, b) for b in range(5)]
+    total = len(work)
+
+    def forwarded(t):
+        for a in range(t * quarter, (t + 1) * quarter):
+            g_f(YB, a).wait_recv()
+        score(FB, t)
+
     for i in range(CHUNKS + 1):
         if i < CHUNKS:
             g_y(i).wait_recv()
@@ -179,22 +199,16 @@
             def _():
                 g_f(ZB, i - 1).start()
 
-        for f in work[i * per_step:(i + 1) * per_step]:
+        for f in work[min(i, CHUNKS - 1) * total // (CHUNKS - 1):min(i + 1, CHUNKS - 1) * total // (CHUNKS - 1)]:
             f()
-        if i == half - 1:
-            score(YB, 0)
-        if i == half:
-            score(ZB, 0)
-        if i == half + 1:
-            for a in range(half):
-                g_f(YB, a).wait_recv()
-            score(FB, 0)
-        if i == CHUNKS - 1:
-            score(YB, 1)
-    score(ZB, 1)
-    for a in range(half, CHUNKS):
-        g_f(YB, a).wait_recv()
-    score(FB, 1)
+        t, phase = divmod(i + 1, quarter)
+        if phase == 0 and i < CHUNKS:
+            score(YB, t - 1)
+        if phase == 1 and t:
+            score(ZB, t - 1)
+        if phase == 2 and t:
+            forwarded(t - 1)
+    forwarded(BANDS - 1)
     for i in range(CHUNKS):
         g_y(i).wait_send()
         g_sib(i).wait_send()
@@ -220,22 +234,20 @@
     loss[...] = (dt - cross) / zt - jnp.log(zt) + jnp.log(zs)
     ks, kt = scale / zs, scale / zt
 
-    def make_grads(b, j):
-        def one(t, _):
-            r = pl.ds(pl.multiple_of(j * size + t * 64, 64), 64)
+    def weigh(b, start, count):
+        def grads(t, _):
+            r = pl.ds(pl.multiple_of(start + t * 64, 64), 64)
             h, l = split(st[b, r, :] * ks - tg[b, r, :] * kt)
             gh[b, r, :] = h
             gl[b, r, :] = l
             return 0
-        lax.fori_loop(0, size // 64, one, 0)
-
-    def weigh(b, j):
-        make_grads(b, j)
-        out = pg.at[group(j)] if b == OWN else win.at[b, group(j)]
+        lax.fori_loop(0, count // 64, grads, 0)
+        at = pl.ds(start, count)
+        out = pg.at[at] if b == OWN else win.at[b, at]
 
         def one(t, _):
             c = pl.ds(pl.multiple_of(t * 256, 256), 256)
-            out[:, c] = dot3(gh[b, group(j), :], gl[b, group(j), :], qh[:, c], ql[:, c], 1, 0)
+            out[:, c] = dot3(gh[b, at, :], gl[b, at, :], qh[:, c], ql[:, c], 1, 0)
             return 0
         lax.fori_loop(0, width // 256, one, 0)
 
@@ -246,32 +258,30 @@
             return 0
         lax.fori_loop(0, count // 16, one, 0)
 
-    for j in range(2):
-        mine = range(j * half, (j + 1) * half)
-        weigh(FB, j)
+    for t in range(BANDS):
+        mine = range(t * quarter, (t + 1) * quarter)
+        weigh(FB, t * band, band)
         for i in mine:
             t_f(i).start()
-        weigh(ZB, j)
+        weigh(ZB, t * band, band)
 
         @pl.when(z_gets)
         def _():
             for i in mine:
                 t_f(i).wait_recv()
-            add(win.at[ZB], rec.at[FB], j * size, size)
+            add(win.at[ZB], rec.at[FB], t * band, band)
 
         for i in mine:
             t_z(i).start()
-    for j in range(2):
-        mine = range(j * half, (j + 1) * half)
-        weigh(YB, j)
-
-        @pl.when(jnp.logical_not(z_gets))
-        def _():
-            for i in mine:
-                t_f(i).wait_recv()
-            add(win.at[YB], rec.at[FB], j * size, size)
-
-    def query_part(b, m):
+        weigh(YB, t * band, band)
+
+    @pl.when(jnp.logical_not(z_gets))
+    def _():
+        for i in range(CHUNKS):
+            t_f(i).wait_recv()
+        add(win.at[YB], rec.at[FB], 0, rows)
+
+    def query_part(b, m, side):
         def one(t, _):
             c = pl.ds(pl.multiple_of(t * 256, 256), 256)
             x = dot3(gh[b, :, group(m)], gl[b, :, group(m)], wh[b, :, c], wl[b, :, c], 0, 0)
@@ -280,38 +290,46 @@
             else:
                 qg[group(m), c] = qg[group(m), c] + x
             return 0
-        lax.fori_loop(0, width // 256, one, 0)
-
-    def sibling_out():
-        for j in range(2):
-            weigh(SIB, j)
-            for i in range(j * half, (j + 1) * half):
-                t_sib(i).start()
-
-    def own_out():
-        for j in range(2):
-            weigh(OWN, j)
+        tiles = width // 512
+        lax.fori_loop(side * tiles, (side + 1) * tiles, one, 0)
+
+    def sibling_out(j):
+        weigh(SIB, j * size, size)
+        for i in range(j * CHUNKS // 2, (j + 1) * CHUNKS // 2):
+            t_sib(i).start()
 
     def sibling_in():
         for i in range(CHUNKS):
             t_sib(i).wait_recv()
         add(pg, rec.at[SIB], 0, rows)
 
-    work = [sibling_out, own_out] + [
-        functools.partial(query_part, b, m) for b in range(5) for m in range(2)
+    stored = lambda i: pltpu.make_async_copy(pg.at[piece(i)], pout.at[piece(i)], outs.at[i])
+    query_stored = pltpu.make_async_copy(qg, qout, outs.at[CHUNKS])
+
+    work = [functools.partial(sibling_out, j) for j in range(2)]
+    work += [functools.partial(weigh, OWN, j * size, size) for j in range(2)]
+    work += [sibling_in] + [
+        functools.partial(query_part, b, m, side)
+        for b in range(5) for m in range(groups) for side in range(2)
     ]
-    work.insert(4, sibling_in)
-    per_step = -(-len(work) // CHUNKS)
-    for i in range(CHUNKS + 1):
+    work += [query_stored.start]
+    total = len(work)
+    lag = 2
+    for i in range(CHUNKS + lag):
         if i < CHUNKS:
             t_z(i).wait_recv()
             add(win.at[YB], rec.at[ZB], i * step, step)
             t_y(i).start()
-        for f in work[i * per_step:(i + 1) * per_step]:
-            f()
-        if i >= 1:
-            t_y(i - 1).wait_recv()
-            add(pg, rec.at[YB], (i - 1) * step, step)
+        if i < CHUNKS - 1:
+            for f in work[i * total // (CHUNKS - 1):(i + 1) * total // (CHUNKS - 1)]:
+                f()
+        if i >= lag:
+            t_y(i - lag).wait_recv()
+            add(pg, rec.at[YB], (i - lag) * step, step)
+            stored(i - lag).start()
+    query_stored.wait()
+    for i in range(CHUNKS):
+        stored(i).wait()
     for i in range(CHUNKS):
         t_sib(i).wait_send()
         t_f(i).wait_send()
@@ -322,6 +340,7 @@
 def body(n, queries, passages, pattern, teacher):
     rows, width = queries.shape
     vmem = pl.BlockSpec(memory_space=pltpu.VMEM)
+    hbm = pl.BlockSpec(memory_space=pl.ANY)
     loss, query_grad, passage_grad = pl.pallas_call(
         functools.partial(kernel, n),
         out_shape=(
@@ -329,9 +348,14 @@
             jax.ShapeDtypeStruct((rows, width), F32),
             jax.ShapeDtypeStruct((rows, width), F32),
         ),
-        in_specs=[pl.BlockSpec(memory_space=pltpu.SMEM), vmem, vmem, vmem],
-        out_specs=(vmem, vmem, vmem),
+        in_specs=[pl.BlockSpec(memory_space=pltpu.SMEM), hbm, hbm, hbm],
+        out_specs=(vmem, hbm, hbm),
         scratch_shapes=[
+            pltpu.VMEM((rows, width), F32),
+            pltpu.VMEM((rows, width), F32),
+            pltpu.VMEM(teacher.shape, BF16),
+            pltpu.VMEM((rows, width), F32),
+            pltpu.VMEM((rows, width), F32),
             pltpu.VMEM((4, rows, width), F32),
             pltpu.VMEM((5, rows, width), BF16),
             pltpu.VMEM((5, rows, width), BF16),
@@ -349,6 +373,8 @@
             pltpu.SemaphoreType.DMA((4, CHUNKS)),
             pltpu.SemaphoreType.DMA((4, CHUNKS)),
             pltpu.SemaphoreType.DMA((4, CHUNKS)),
+            pltpu.SemaphoreType.DMA((3,)),
+            pltpu.SemaphoreType.DMA((CHUNKS + 1,)),
         ],
         compiler_params=pltpu.CompilerParams(
             collective_id=0, has_side_effects=True, vmem_limit_bytes=60 * 2**20

time: 135 us -> 131 us (0.970)
  Pallas kernels: 127 us -> 123 us
    pallas_call x1, Pallas kernels: 127 us -> 123 us  [body(): pl.pallas_call(functools.partial(kernel, n), out_shape=(jax.ShapeDtypeStr...]
where the time goes in v2:
time: 131 us; the launch traced here: 129 us
  Pallas kernels  123 us (94%)
  local copies, waits for them, and re-layouts  5.88 us (4%)
    pallas_call x1, Pallas kernels, body(): pl.pallas_call(functools.partial(kernel, n), out_shape=(jax.ShapeDtypeStr...  123 us
    unnamed x5, local copies, waits for them, and re-layouts  5.88 us

profile of v2, /device:TPU:1, one launch (start us, length us, event | category | flops | bytes accessed | tf_op | source)
XLA Modules:
  0.0 129.3 jit_solution(7921808699814360346)
XLA Ops:
  0.6 122.8 %shard_map.67 = (f32[1,512]{1,0:T(1,128)}, f32[512,1024]{1,0:T(8,128)}, f32[512,1024]{1,0:T(8,128)}) custom-call(s32[2,8]{1,0:T(2,128)} %pat.1, f32[512,1024]{1,0:T(8,128)} %qin.1, f32[512,1024]{1,0:T(8,128)} %pin.1, bf16[2,8,256,256]{3,2,1,0:T(8,128)(2,1)} %tin.1), custom_call_target="tpu_custom_call" | custom-call | tf_op jit(solution)/shard_map/pallas_call | solution.py:344
  123.4 1.3 copy.10
  124.7 0.0 copy-start
  124.7 3.3 %copy.11 = f32[512,1024]{1,0:T(8,128)} copy(f32[512,1024]{1,0:T(8,128)} %get-tuple-element.13) | data formatting | bytes 4194304
  128.0 0.0 copy-done
  128.0 1.3 %copy.12 = f32[512,1024]{1,0:T(8,128)} copy(f32[512,1024]{1,0:T(8,128)S(1)} %copy-done) | data formatting | bytes 4194304
Async XLA Ops:
  124.7 3.3 %copy-start = (f32[512,1024]{1,0:T(8,128)S(1)}, f32[512,1024]{1,0:T(8,128)}, u32[]{:S(2)}) copy-start(f32[512,1024]{1,0:T(8,128)} %get-tuple-element.14) | copy-start | bytes 6291460
